TPU v7x, 32 devices: a whole 2x2x4 slice. The times are simulated.
32 devices in a mesh: groups: 2 (over y), dict: 16 (over z, x, core).
Axes of the slice: x: 2, y: 2, z: 4, core: 2. Of those that a mesh axis runs over, the one named last changes fastest.
Arguments:
- activations: bfloat16 [4096, 3584], P(('groups', 'dict')), parts along dimension 0, may hold values from -6 to 6
- block_ids: int32 [4096, 32], P(('groups', 'dict')), parts along dimension 0, may hold values from 0 to 63, as said below
- slot_mask: int32 [4096, 32], P(('groups', 'dict')), parts along dimension 0, may hold values from 0 to 1
- enc_weight: bfloat16 [3584, 4096], P(None, 'dict'), may hold values from -0.09375 to 0.09375
- enc_bias: float32 [4096], P('dict'), may hold values from -3 to 3
- dec_weight: bfloat16 [4096, 3584], P('dict'), may hold values from -0.75 to 0.75
- dec_bias: float32 [3584], replicated, may hold values from -3 to 3
Outputs:
- recon_error: bfloat16 [4096, 3584], P(('groups', 'dict')), parts along dimension 0
- grad_enc: float32 [7168, 4096], P('groups', 'dict'), parts along dimension 0
- grad_enc_bias: float32 [8192], P(('groups', 'dict')), parts along dimension 0
- grad_dec: float32 [8192, 3584], P(('groups', 'dict')), parts along dimension 0
- grad_dec_bias: float32 [7168], P('groups'), parts along dimension 0
There are 2 independent parts, one for each index of `groups`. A program takes and returns all parts, laid end to end along the dimension named above; an argument that names none is the same for every part. Nothing has to cross between parts.
Inputs may be any that keep to these rules, and one draw needn't show every extreme that they name: `block_ids`: slot k of a row names one of the blocks k * 2 to (k + 1) * 2 - 1, so a row's blocks are distinct. Among the rows of one device (aligned blocks of 128 rows) each block is named by at most 2 live slots, and in every draw some block is named by exactly 2 live slots on every device. Slots that are not live carry nothing.
All inputs are finite; a program needn't handle non-finite values.
Results may differ from a plain program's by a relative error of at most 0.0049.
Values may be sent and summed in bfloat16 or wider, within the bound.
A program may use at most 128 MiB of HBM per device.

v0:
```python
import jax
import jax.numpy as jnp
from jax import lax
from jax.sharding import PartitionSpec as P

BLOCK = 64
CAP = 2
ROW_DEV = 128


def body(activations, block_ids, slot_mask, enc_weight, enc_bias, dec_weight, dec_bias):
    devices = lax.axis_size("dict")
    model_width = activations.shape[1]
    local_blocks = enc_bias.shape[0] // BLOCK
    all_blocks = local_blocks * devices
    slot_total = all_blocks * CAP
    norm_scale = 1.0 / ROW_DEV
    is_live = slot_mask == 1
    block_range = jnp.arange(all_blocks, dtype=jnp.int32)
    row_hits = jnp.sum(
        ((block_ids[:, :, None] == block_range[None, None, :]) & is_live[:, :, None]).astype(
            jnp.int32
        ),
        axis=1,
    )
    earlier = jnp.cumsum(row_hits, axis=0) - row_hits
    slot_rank = jnp.take_along_axis(earlier, block_ids, axis=1)
    position = block_ids * CAP + slot_rank
    matches = (
        position[:, :, None] == jnp.arange(slot_total, dtype=jnp.int32)[None, None, :]
    ) & is_live[:, :, None]
    assign_bool = jnp.any(matches, axis=1)
    assign = assign_bool.astype(jnp.bfloat16)
    slot_flags = (
        jnp.any(assign_bool, axis=0).astype(jnp.bfloat16).reshape(devices, local_blocks, CAP)
    )
    outgoing = jnp.einsum("rp,rd->pd", assign, activations, preferred_element_type=jnp.float32)
    outgoing = outgoing.astype(jnp.bfloat16).reshape(devices, local_blocks, CAP, model_width)
    enc_blocks = enc_weight.reshape(model_width, local_blocks, BLOCK)
    dec_blocks = dec_weight.reshape(local_blocks, BLOCK, model_width)
    bias_blocks = enc_bias.reshape(local_blocks, BLOCK)
    rows_in = lax.all_to_all(outgoing, "dict", split_axis=0, concat_axis=0, tiled=True)
    flags_in = lax.all_to_all(slot_flags, "dict", split_axis=0, concat_axis=0, tiled=True)
    preact = jnp.einsum("sbcd,dbl->sbcl", rows_in, enc_blocks, preferred_element_type=jnp.float32)
    preact = preact + bias_blocks[None, :, None, :]
    latent = jnp.where(flags_in[..., None] > 0, jnp.maximum(preact, 0.0), 0.0).astype(jnp.bfloat16)
    partial_terms = jnp.einsum(
        "sbcl,bld->sbcd", latent, dec_blocks, preferred_element_type=jnp.float32
    )
    returned = lax.all_to_all(
        partial_terms.astype(jnp.bfloat16), "dict", split_axis=0, concat_axis=0, tiled=True
    )
    result = (returned, rows_in, latent)
    returned, rows_kept, latent_kept = result
    combined = jnp.dot(
        assign, returned.reshape(slot_total, model_width), preferred_element_type=jnp.float32
    )
    residual = combined + dec_bias[None, :] - activations.astype(jnp.float32)
    recon_error = residual.astype(jnp.bfloat16)
    grad_dec_bias = lax.psum(norm_scale * jnp.sum(residual, axis=0), "dict")
    err_out = jnp.einsum("rp,rd->pd", assign, recon_error, preferred_element_type=jnp.float32)
    err_out = err_out.astype(jnp.bfloat16).reshape(devices, local_blocks, CAP, model_width)
    err_in = lax.all_to_all(err_out, "dict", split_axis=0, concat_axis=0, tiled=True)
    rows_in = rows_kept
    latent = latent_kept
    grad_dec = norm_scale * jnp.einsum(
        "sbcl,sbcd->bld", latent, err_in, preferred_element_type=jnp.float32
    )
    grad_dec = grad_dec.reshape(local_blocks * BLOCK, model_width)
    dlatent = norm_scale * jnp.einsum(
        "sbcd,bld->sbcl", err_in, dec_blocks, preferred_element_type=jnp.float32
    )
    dlatent = jnp.where(latent > 0, dlatent, 0.0)
    grad_enc_bias = jnp.sum(dlatent, axis=(0, 2)).reshape(local_blocks * BLOCK)
    grad_enc = jnp.einsum(
        "sbcd,sbcl->dbl", rows_in, dlatent.astype(jnp.bfloat16), preferred_element_type=jnp.float32
    )
    grad_enc = grad_enc.reshape(model_width, local_blocks * BLOCK)
    return (recon_error, grad_enc, grad_enc_bias, grad_dec, grad_dec_bias)


def solution(mesh):
    return jax.shard_map(
        body,
        mesh=mesh,
        in_specs=(
            P(("groups", "dict"), None),
            P(("groups", "dict"), None),
            P(("groups", "dict"), None),
            P(None, "dict"),
            P("dict"),
            P("dict", None),
            P(),
        ),
        out_specs=(
            P(("groups", "dict"), None),
            P("groups", "dict"),
            P(("groups", "dict")),
            P(("groups", "dict"), None),
            P("groups"),
        ),
        check_vma=False,
    )
```

profile of v0, /device:TPU:0, one launch (start us, length us, event | category | flops | bytes accessed | tf_op | source)
XLA Modules:
  0.0 197.1 jit_solution(4187447880411673253)
XLA Ops:
  0.6 0.9 broadcast_compare_fusion
  2.2 0.9 convert_reduce_fusion
  3.7 26.7 %gather_fusion = s32[4096]{0:T(1024)S(1)} fusion(s32[128,64]{1,0:T(8,128)S(1)} %sub.6, s32[4096]{0:T(1024)S(1)} %reshape.64), kind=kCustom, calls=%fused_computation | custom fusion | bytes 65536 | tf_op jit(solution)/shard_map/jit(take_along_axis)/gather | solution.py:27
  30.7 1.4 fusion.4
  32.3 0.8 copy.72
  33.2 7.4 %all-to-all-start = ((bf16[16,4,2]{1,2,0:T(2,128)(2,1)}), bf16[16,4,2]{1,2,0:T(2,128)(2,1)S(1)}, u32[]{:S(2)}, u32[]{:S(2)}) async-start(bf16[16,4,2]{1,2,0:T(2,128)(2,1)} %copy.72), calls=%async_computation | async-start | bytes 16384 | tf_op jit(solution)/shard_map/all_to_all | solution.py:43
  40.5 1.6 convolution_convert_fusion.2
  42.2 1.3 reshape.55
  43.4 3.4 %all-to-all-done = bf16[16,4,2]{1,2,0:T(2,128)(2,1)S(1)} async-done(((bf16[16,4,2]{1,2,0:T(2,128)(2,1)}), bf16[16,4,2]{1,2,0:T(2,128)(2,1)S(1)}, u32[]{:S(2)}, u32[]{:S(2)}) %all-to-all-start) | async-done | bytes 288 | tf_op jit(solution)/shard_map/all_to_all | solution.py:43
  46.9 3.6 %all-to-all-start.1 = ((bf16[16,4,2,3584]{3,2,1,0:T(2,128)(2,1)}), bf16[16,4,2,3584]{3,2,1,0:T(2,128)(2,1)S(1)}, u32[]{:S(2)}, u32[]{:S(2)}) async-start(bf16[16,4,2,3584]{3,2,1,0:T(2,128)(2,1)} %reshape.55), calls=%async_computation.1 | async-start | bytes 1835008 | tf_op jit(solution)/shard_map/all_to_all | solution.py:42
  50.5 3.8 %copy.75 = bf16[3584,256]{0,1:T(8,128)(2,1)} copy(bf16[3584,256]{1,0:T(8,128)(2,1)} %param.10) | data formatting | bytes 3670016 | tf_op args[3]
  54.5 16.7 %all-to-all-done.1 = bf16[16,4,2,3584]{3,2,1,0:T(2,128)(2,1)S(1)} async-done(((bf16[16,4,2,3584]{3,2,1,0:T(2,128)(2,1)}), bf16[16,4,2,3584]{3,2,1,0:T(2,128)(2,1)S(1)}, u32[]{:S(2)}, u32[]{:S(2)}) %all-to-all-start.1) | async-done | bytes 917536 | tf_op jit(solution)/shard_map/all_to_all | solution.py:42
  71.3 2.5 %fusion.11 = bf16[16,4,2,64]{3,0,2,1:T(8,128)(2,1)S(1)} fusion(bf16[3584,4,64,1]{0,2,3,1:T(8,128)(2,1)} %bitcast.54, bf16[16,4,2,3584]{3,2,1,0:T(2,128)(2,1)S(1)} %all-to-all-done.1, f32[4,64]{1,0:T(4,128)S(1)} %add.35, pred[16,4,2]{0,2,1:T(4,128)(4,1)S(1)} %copy.74), kind=kOutput, calls=%fused_computation.20 | convolution fusion | flops 58753024 | bytes 2770048 | tf_op jit(solution)/shard_map/sbcd,dbl->sbcl/dot_general | solution.py:44
  74.2 0.9 copy.77
  75.1 28.5 %all_to_all.20 = bf16[16,4,2,3584]{3,2,1,0:T(2,128)(2,1)S(1)} all-to-all(bf16[16,4,2,3584]{3,2,1,0:T(2,128)(2,1)S(1)} %copy.77), channel_id=1, replica_groups=mesh['groups'=2,'dict'=16] {'dict'}, dimensions={0} | all-to-all | bytes 1835008 | tf_op jit(solution)/shard_map/all_to_all | solution.py:50
  103.6 1.3 reshape.58
  104.9 1.9 fusion.19
  106.8 0.9 copy-done.3
  108.2 1.3 reshape.59
  109.4 4.5 %all-to-all-start.3 = ((bf16[16,4,2,3584]{3,2,1,0:T(2,128)(2,1)}), bf16[16,4,2,3584]{3,2,1,0:T(2,128)(2,1)S(1)}, u32[]{:S(2)}, u32[]{:S(2)}) async-start(bf16[16,4,2,3584]{3,2,1,0:T(2,128)(2,1)} %reshape.59), calls=%async_computation.3 | async-start | bytes 1835008 | tf_op jit(solution)/shard_map/all_to_all | solution.py:63
  113.9 71.2 %psum.7 = f32[3584]{0:T(1024)} all-reduce(f32[3584]{0:T(1024)S(1)} %broadcast_multiply_fusion), channel_id=1, replica_groups=mesh['groups'=2,'dict'=16] {'dict'}, use_global_device_ids=true, to_apply=%region_6.7 | all-reduce | flops 3584 | bytes 28672 | tf_op jit(solution)/shard_map/psum | solution.py:60
  186.3 2.5 %fusion.15 = f32[4,64,3584,1]{2,1,3,0:T(8,128)} fusion(bf16[16,4,2,3584]{3,2,1,0:T(2,128)(2,1)S(1)} %copy-done.2, bf16[16,4,2,64]{3,0,2,1:T(8,128)(2,1)S(1)} %get-tuple-element.36), kind=kOutput, calls=%fused_computation.26 | convolution fusion | flops 58720256 | bytes 4603904 | tf_op jit(solution)/shard_map/sbcd,sbcl->dbl/dot_general | solution.py:75
  188.8 5.1 %copy.81 = f32[3584,256]{1,0:T(8,128)} copy(f32[3584,256]{0,1:T(8,128)} %bitcast.52) | data formatting | bytes 7340032
  194.6 2.5 %fusion = f32[4,64,3584]{2,1,0:T(8,128)} fusion(bf16[16,4,2,64]{3,0,2,1:T(8,128)(2,1)S(1)} %fusion.11, bf16[16,4,2,3584]{3,2,1,0:T(2,128)(2,1)S(1)} %all-to-all-done.3), kind=kOutput, calls=%fused_computation.2 | convolution fusion | flops 59637760 | bytes 4603904 | tf_op jit(solution)/shard_map/sbcl,sbcd->bld/dot_general | solution.py:66
  (36 shorter events, 4.6 us)
Async XLA Ops:
  0.6 73.1 %copy-start = (bf16[256,3584]{1,0:T(8,128)(2,1)S(1)}, bf16[256,3584]{1,0:T(8,128)(2,1)}, u32[]{:S(2)}) copy-start(bf16[256,3584]{1,0:T(8,128)(2,1)} %param.12) | copy-start | bytes 5505028
  3.7 26.9 %copy-start.4 = (s32[128,32]{0,1:T(8,128)S(1)}, s32[128,32]{0,1:T(8,128)}, u32[]{:S(2)}) copy-start(s32[128,32]{0,1:T(8,128)} %param.8) | copy-start | bytes 49156
  33.2 13.7 %all-to-all-start = ((bf16[16,4,2]{1,2,0:T(2,128)(2,1)}), bf16[16,4,2]{1,2,0:T(2,128)(2,1)S(1)}, u32[]{:S(2)}, u32[]{:S(2)}) async-start(bf16[16,4,2]{1,2,0:T(2,128)(2,1)} %copy.72), calls=%async_computation | async-start | bytes 16384 | tf_op jit(solution)/shard_map/all_to_all | solution.py:43
  46.9 24.4 %all-to-all-start.1 = ((bf16[16,4,2,3584]{3,2,1,0:T(2,128)(2,1)}), bf16[16,4,2,3584]{3,2,1,0:T(2,128)(2,1)S(1)}, u32[]{:S(2)}, u32[]{:S(2)}) async-start(bf16[16,4,2,3584]{3,2,1,0:T(2,128)(2,1)} %reshape.55), calls=%async_computation.1 | async-start | bytes 1835008 | tf_op jit(solution)/shard_map/all_to_all | solution.py:42
  50.5 3.8 %copy-start.6 = (f32[256]{0:T(256)S(1)}, f32[256]{0:T(256)}, u32[]{:S(2)}) copy-start(f32[256]{0:T(256)} %param.11) | copy-start | bytes 3076
  71.3 2.9 %copy-start.1 = (bf16[16,4,2,3584]{3,2,1,0:T(2,128)(2,1)}, bf16[16,4,2,3584]{3,2,1,0:T(2,128)(2,1)S(1)}, u32[]{:S(2)}) copy-start(bf16[16,4,2,3584]{3,2,1,0:T(2,128)(2,1)S(1)} %all-to-all-done.1) | copy-start | bytes 2752516
  75.1 29.8 %copy-start.5 = (f32[3584]{0:T(1024)S(1)}, f32[3584]{0:T(1024)}, u32[]{:S(2)}) copy-start(f32[3584]{0:T(1024)} %param.13) | copy-start | bytes 43012
  106.8 0.9 copy-start.3
  109.4 75.7 %all-to-all-start.3 = ((bf16[16,4,2,3584]{3,2,1,0:T(2,128)(2,1)}), bf16[16,4,2,3584]{3,2,1,0:T(2,128)(2,1)S(1)}, u32[]{:S(2)}, u32[]{:S(2)}) async-start(bf16[16,4,2,3584]{3,2,1,0:T(2,128)(2,1)} %reshape.59), calls=%async_computation.3 | async-start | bytes 1835008 | tf_op jit(solution)/shard_map/all_to_all | solution.py:63
  185.1 1.2 copy-start.2
where the time goes:
time: 198 us; the launch traced here: 197 us
  blocking collectives  99.6 us (50%)
  local copies, waits for them, and re-layouts  44.3 us (22%)
  waiting for transfers between devices  20.2 us (10%)
  starting transfers between devices  15.5 us (8%)
  matrix products  12.5 us (6%)
  other arithmetic  4.17 us (2%)
    psum x1, blocking collectives, body(): grad_dec_bias = lax.psum(norm_scale * jnp.sum(residual, axis=0), 'dict')  71.2 us
    all_to_all x1, blocking collectives, body(): lax.all_to_all(partial_terms.astype(jnp.bfloat16), 'dict', split_axis=0,...  28.5 us
    gather x5, local copies, waits for them, and re-layouts, body(): slot_rank = jnp.take_along_axis(earlier, block_ids, axis=1)  27 us
    all_to_all x1, waiting for transfers between devices, body(): lax.all_to_all(outgoing, 'dict', split_axis=0, concat_axis=0, tiled=True)  16.7 us
    unnamed x16, local copies, waits for them, and re-layouts  10.4 us
    all_to_all x1, starting transfers between devices, body(): lax.all_to_all(slot_flags, 'dict', split_axis=0, concat_axis=0, tiled=True)  7.36 us
    all_to_all x1, starting transfers between devices, body(): lax.all_to_all(err_out, 'dict', split_axis=0, concat_axis=0, tiled=True)  4.47 us
  transfers between devices with their start and end apart: 3, of which 2 were waited for; matrix products, arithmetic and copies ran while one was open for 4% of the time, Pallas kernels for 0%

commit v1 on v0

v1 whole, which is shorter than its diff:
```python
import functools

import jax
import jax.numpy as jnp
from jax import lax
from jax.experimental import pallas as pl
from jax.experimental.pallas import tpu as pltpu
from jax.sharding import PartitionSpec as P

BLOCK = 64
CAP = 2
ROW_DEV = 128
SCALE = 1.0 / ROW_DEV
LANES = 128
VMEM_LIMIT = 58 * 1024 * 1024
F32 = jnp.float32
BF16 = jnp.bfloat16


def chunk_list(half):
    units = half // LANES
    parts = [4, 4, 4] if units > 12 else []
    rest = units - sum(parts)
    parts = ([rest] if rest else []) + parts
    out, start = [], 0
    for part in parts:
        out.append((start * LANES, part * LANES))
        start += part
    return out


def dot(a, b):
    return jnp.dot(a, b, preferred_element_type=F32)


def dot_nt(a, b):
    return lax.dot_general(a, b, (((1,), (1,)), ((), ())), preferred_element_type=F32)


def dot_tn(a, b):
    return lax.dot_general(a, b, (((0,), (0,)), ((), ())), preferred_element_type=F32)


def exchange_kernel(
    n, slots, ids_ref, live_ref, act_ref, enc_bias_ref, dec_bias_ref, enc_hbm, dec_hbm,
    recon_ref, rows_hbm, err_hbm, lat_ref, dlat_ref, enc_grad_ref, sum_ref,
    enc, dec, out_buf, rows_in, term_out, term_in, err_in, pick, pick_t, part, part_in,
    load_sem, store_sem, send1, recv1, send2, recv2, send3, recv3, send4, recv4,
):
    me = lax.axis_index("dict")
    rows_total = 16 * n
    rows = act_ref.shape[0]
    half = act_ref.shape[1] // 2
    width = BLOCK * 4
    chunks = chunk_list(half)
    bits = [1 << k for k in range(n.bit_length() - 1)]

    def peer_of(step):
        index = n - step
        return sum(((me // bit + index // bit) % 2) * bit for bit in bits)

    def for_peers(fn):
        def step_fn(step, carry):
            fn(peer_of(step))
            return carry

        lax.fori_loop(1, n, step_fn, 0)

    barrier = pltpu.get_barrier_semaphore()
    for_peers(
        lambda peer: pl.semaphore_signal(
            barrier, inc=1, device_id={"dict": peer}, device_id_type=pl.DeviceIdType.MESH
        )
    )
    enc_load = pltpu.make_async_copy(enc_hbm, enc, load_sem.at[0])
    dec_load = pltpu.make_async_copy(dec_hbm, dec, load_sem.at[1])
    enc_load.start()
    dec_load.start()

    def block_rows(device):
        return pl.ds(pl.multiple_of(device * 16, 16), 16)

    def send(src, dst, start, size, send_sem, recv_sem):
        mine = block_rows(me)
        columns = pl.ds(start, size)

        def one(peer):
            pltpu.make_async_remote_copy(
                src_ref=src.at[block_rows(peer), columns],
                dst_ref=dst.at[mine, columns],
                send_sem=send_sem,
                recv_sem=recv_sem,
                device_id={"dict": peer},
                device_id_type=pl.DeviceIdType.MESH,
            ).start()

        for_peers(one)
        dst[mine, columns] = src[mine, columns]

    def wait_all(buf, start, size, sem):
        view = buf.at[pl.ds(0, (n - 1) * 16), pl.ds(start, size)]
        pltpu.make_async_copy(view, view, sem).wait()

    column = lax.broadcasted_iota(jnp.int32, (slots, rows_total), 1)
    block = (column // 16) * 4 + (column % 8) // CAP
    per_slot = 4 * n // slots
    spread = (
        lax.broadcasted_iota(jnp.int32, (slots, rows_total), 0) == block // per_slot
    ).astype(F32).astype(BF16)
    slot_base = lax.broadcasted_iota(jnp.int32, (rows, slots), 1) * per_slot
    code = jnp.where(live_ref[...] == 1, ids_ref[...] - slot_base + 1, 0).astype(F32)
    code = dot(code.astype(BF16), spread)
    column = lax.broadcasted_iota(jnp.int32, (rows, rows_total), 1)
    block = (column // 16) * 4 + (column % 8) // CAP
    hit = code == (block % per_slot + 1).astype(F32)
    lower = (
        lax.broadcasted_iota(jnp.int32, (rows, rows), 1)
        < lax.broadcasted_iota(jnp.int32, (rows, rows), 0)
    ).astype(F32).astype(BF16)
    earlier = dot(lower, hit.astype(F32).astype(BF16))
    chosen = hit & (earlier == (column % CAP).astype(F32))
    top = (column // 8) % 2
    pick_low = jnp.where(chosen & (top == 0), 1.0, 0.0)
    pick_high = jnp.where(chosen & (top == 1), 1.0, 0.0)
    both = jnp.concatenate([pick_low, pick_high], axis=0)
    pick[...] = both.astype(BF16)
    pick_t[...] = both.T.astype(BF16)

    for start, size in chunks:
        stacked = jnp.concatenate(
            [act_ref[:, start : start + size], act_ref[:, half + start : half + start + size]],
            axis=0,
        )
        out_buf[:, start : start + size] = dot(pick_t[...], stacked).astype(BF16)

    pl.semaphore_wait(barrier, n - 1)
    send(out_buf, rows_in, 0, half, send1, recv1)
    enc_load.wait()
    wait_all(rows_in, 0, half, recv1)

    low = dot(rows_in[...], enc[:half, :]).reshape(n, 2, 8, width)
    high = dot(rows_in[...], enc[half:, :]).reshape(n, 2, 8, width)
    preact = low[:, 0] + high[:, 1] + enc_bias_ref[...].reshape(1, 1, width)
    own_block = (
        lax.broadcasted_iota(jnp.int32, (n, 8, width), 1) // CAP
        == lax.broadcasted_iota(jnp.int32, (n, 8, width), 2) // BLOCK
    )
    latent = jnp.where(own_block, jnp.maximum(preact, 0.0), 0.0)

    def stack(value):
        value = jnp.broadcast_to(value[:, None], (n, 2, 8, width))
        return value.reshape(rows_total, width)

    latent_both = stack(latent)
    lat_ref[...] = latent_both.astype(BF16)
    live_top = (lax.broadcasted_iota(jnp.int32, (rows_total, width), 0) // 8) % 2
    latent_low = jnp.where(live_top == 0, latent_both, 0.0).astype(BF16)
    latent_high = jnp.where(live_top == 1, latent_both, 0.0).astype(BF16)

    dec_load.wait()
    for c, (start, size) in enumerate(chunks):
        value = dot(latent_low, dec[:, start : start + size])
        value = value + dot(latent_high, dec[:, half + start : half + start + size])
        term_out[:, start : start + size] = value.astype(BF16)
        send(term_out, term_in, start, size, send2.at[c], recv2.at[c])

    rows_store = pltpu.make_async_copy(rows_in, rows_hbm, store_sem.at[0])
    rows_store.start()
    wait_all(out_buf, 0, half, send1)

    units_per = part.shape[1]
    part[...] = jnp.zeros_like(part)
    for c, (start, size) in enumerate(chunks):
        wait_all(term_in, start, size, recv2.at[c])
        combined = dot(pick[...], term_in[:, start : start + size])
        errors = []
        for h in range(2):
            first = h * half + start
            residual = combined[h * rows : (h + 1) * rows]
            residual = residual + dec_bias_ref[:, first : first + size]
            residual = residual - act_ref[:, first : first + size].astype(F32)
            error = residual.astype(BF16)
            recon_ref[:, first : first + size] = error
            errors.append(error)
            total = SCALE * jnp.sum(residual, axis=0, keepdims=True)
            for u in range(size // LANES):
                unit = first // LANES + u
                part[unit // units_per, unit % units_per, :] = total[
                    0, u * LANES : (u + 1) * LANES
                ]
        out_buf[:, start : start + size] = dot(
            pick_t[...], jnp.concatenate(errors, axis=0)
        ).astype(BF16)
        send(out_buf, err_in, start, size, send3.at[c], recv3.at[c])

    def send_part(peer):
        pltpu.make_async_remote_copy(
            src_ref=part.at[peer],
            dst_ref=part_in.at[me],
            send_sem=send4.at[0],
            recv_sem=recv4.at[0],
            device_id={"dict": peer},
            device_id_type=pl.DeviceIdType.MESH,
        ).start()

    for_peers(send_part)
    part_in[me] = part[me]

    def wait_parts(buf, sem):
        view = buf.at[pl.ds(0, n - 1)]
        pltpu.make_async_copy(view, view, sem).wait()

    wait_parts(part_in, recv4.at[0])
    wait_parts(part, send4.at[0])
    sum_ref[me] = jnp.sum(part_in[...], axis=0)

    def send_total(peer):
        pltpu.make_async_remote_copy(
            src_ref=sum_ref.at[me],
            dst_ref=sum_ref.at[me],
            send_sem=send4.at[1],
            recv_sem=recv4.at[1],
            device_id={"dict": peer},
            device_id_type=pl.DeviceIdType.MESH,
        ).start()

    for_peers(send_total)

    low = jnp.zeros((rows_total, width), F32)
    high = jnp.zeros((rows_total, width), F32)
    stores = []
    for c, (start, size) in enumerate(chunks):
        wait_all(err_in, start, size, recv3.at[c])
        columns = pl.ds(start, size)
        store = pltpu.make_async_copy(
            err_in.at[:, columns], err_hbm.at[:, columns], store_sem.at[1 + c]
        )
        store.start()
        stores.append(store)
        value = err_in[:, start : start + size]
        low = low + dot_nt(value, dec[:, start : start + size])
        high = high + dot_nt(value, dec[:, half + start : half + start + size])
    low = low.reshape(n, 2, 8, width)
    high = high.reshape(n, 2, 8, width)
    latent = lat_ref[...].astype(F32).reshape(n, 2, 8, width)[:, 0]
    dlatent = jnp.where(latent > 0, SCALE * (low[:, 0] + high[:, 1]), 0.0)
    enc_grad_ref[...] = jnp.sum(dlatent.reshape(n * 8, width), axis=0, keepdims=True)
    dlat_ref[...] = stack(dlatent).astype(BF16)

    for c, (start, size) in enumerate(chunks):
        wait_all(term_out, start, size, send2.at[c])
        wait_all(out_buf, start, size, send3.at[c])
        stores[c].wait()
    rows_store.wait()
    wait_parts(sum_ref, recv4.at[1])
    wait_parts(sum_ref, send4.at[1])


def grad_kernel(rows_ref, err_ref, lat_ref, dlat_ref, enc_ref, dec_ref):
    h = pl.program_id(0)
    top = (lax.broadcasted_iota(jnp.int32, lat_ref.shape, 0) // 8) % 2
    keep = top == h
    latent = jnp.where(keep, lat_ref[...].astype(F32), 0.0).astype(BF16)
    dlatent = jnp.where(keep, dlat_ref[...].astype(F32), 0.0).astype(BF16)
    enc_ref[...] = dot_tn(rows_ref[...], dlatent)
    dec_ref[...] = SCALE * dot_tn(latent, err_ref[...])


def body(activations, block_ids, slot_mask, enc_weight, enc_bias, dec_weight, dec_bias):
    n = lax.axis_size("dict")
    rows, model_width = activations.shape
    half = model_width // 2
    width = enc_bias.shape[0]
    rows_total = 16 * n
    units = model_width // LANES
    units_per = -(-units // n)
    chunks = len(chunk_list(half))
    vmem = pl.BlockSpec(memory_space=pltpu.VMEM)
    hbm = pl.BlockSpec(memory_space=pl.ANY)
    slot_buf = pltpu.VMEM((rows_total, half), BF16)
    recon_error, rows_in, err_in, latent, dlatent, enc_bias_grad, sums = pl.pallas_call(
        functools.partial(exchange_kernel, n, block_ids.shape[1]),
        out_shape=(
            jax.ShapeDtypeStruct((rows, model_width), BF16),
            jax.ShapeDtypeStruct((rows_total, half), BF16),
            jax.ShapeDtypeStruct((rows_total, half), BF16),
            jax.ShapeDtypeStruct((rows_total, width), BF16),
            jax.ShapeDtypeStruct((rows_total, width), BF16),
            jax.ShapeDtypeStruct((1, width), F32),
            jax.ShapeDtypeStruct((n, units_per, LANES), F32),
        ),
        in_specs=[vmem] * 5 + [hbm] * 2,
        out_specs=(vmem, hbm, hbm, vmem, vmem, vmem, vmem),
        scratch_shapes=[
            pltpu.VMEM((model_width, width), BF16),
            pltpu.VMEM((width, model_width), BF16),
            slot_buf,
            slot_buf,
            slot_buf,
            slot_buf,
            slot_buf,
            pltpu.VMEM((2 * rows, rows_total), BF16),
            pltpu.VMEM((rows_total, 2 * rows), BF16),
            pltpu.VMEM((n, units_per, LANES), F32),
            pltpu.VMEM((n, units_per, LANES), F32),
            pltpu.SemaphoreType.DMA((2,)),
            pltpu.SemaphoreType.DMA((1 + chunks,)),
            pltpu.SemaphoreType.DMA,
            pltpu.SemaphoreType.DMA,
            pltpu.SemaphoreType.DMA((chunks,)),
            pltpu.SemaphoreType.DMA((chunks,)),
            pltpu.SemaphoreType.DMA((chunks,)),
            pltpu.SemaphoreType.DMA((chunks,)),
            pltpu.SemaphoreType.DMA((2,)),
            pltpu.SemaphoreType.DMA((2,)),
        ],
        compiler_params=pltpu.CompilerParams(
            collective_id=0, has_side_effects=True, vmem_limit_bytes=VMEM_LIMIT
        ),
        name="exchange",
    )(
        block_ids,
        slot_mask,
        activations,
        enc_bias.reshape(1, width),
        dec_bias.reshape(1, model_width),
        enc_weight,
        dec_weight,
    )
    tiles = 2
    tile = half // tiles
    grad_enc, grad_dec = pl.pallas_call(
        grad_kernel,
        grid=(2, tiles),
        out_shape=(
            jax.ShapeDtypeStruct((model_width, width), F32),
            jax.ShapeDtypeStruct((width, model_width), F32),
        ),
        in_specs=[
            pl.BlockSpec((rows_total, tile), lambda h, j: (0, j)),
            pl.BlockSpec((rows_total, tile), lambda h, j: (0, j)),
            pl.BlockSpec((rows_total, width), lambda h, j: (0, 0)),
            pl.BlockSpec((rows_total, width), lambda h, j: (0, 0)),
        ],
        out_specs=(
            pl.BlockSpec((tile, width), lambda h, j: (h * tiles + j, 0)),
            pl.BlockSpec((width, tile), lambda h, j: (0, h * tiles + j)),
        ),
        compiler_params=pltpu.CompilerParams(vmem_limit_bytes=VMEM_LIMIT),
        name="grads",
    )(rows_in, err_in, latent, dlatent)
    return (
        recon_error,
        grad_enc,
        enc_bias_grad.reshape(width),
        grad_dec,
        sums.reshape(n * units_per * LANES)[:model_width],
    )


def solution(mesh):
    return jax.shard_map(
        body,
        mesh=mesh,
        in_specs=(
            P(("groups", "dict"), None),
            P(("groups", "dict"), None),
            P(("groups", "dict"), None),
            P(None, "dict"),
            P("dict"),
            P("dict", None),
            P(),
        ),
        out_specs=(
            P(("groups", "dict"), None),
            P("groups", "dict"),
            P(("groups", "dict")),
            P(("groups", "dict"), None),
            P("groups"),
        ),
        check_vma=False,
    )
```

time: 198 us -> 90 us (0.45)
  blocking collectives: 99.6 us -> 0 us
  Pallas kernels: 0 us -> 80.5 us
  local copies, waits for them, and re-layouts: 44.3 us -> 8.28 us
  waiting for transfers between devices: 20.2 us -> 0 us
  starting transfers between devices: 15.5 us -> 0 us
  matrix products: 12.5 us -> 0 us
  other arithmetic: 4.17 us -> 0 us
    pallas_call x0 -> x2, Pallas kernels: none -> 80.5 us  [the longest x1 74.3 us: body(): pl.pallas_call(functools.partial(exchange_kernel, n, block_ids.shape[1]),...]
    psum x1 -> x0, blocking collectives: 71.2 us -> none  [body(): grad_dec_bias = lax.psum(norm_scale * jnp.sum(residual, axis=0), 'dict')]
    all_to_all x1 -> x0, blocking collectives: 28.5 us -> none  [body(): lax.all_to_all(partial_terms.astype(jnp.bfloat16), 'dict', split_axis=0,...]
    gather x5 -> x0, local copies, waits for them, and re-layouts: 27 us -> none  [body(): slot_rank = jnp.take_along_axis(earlier, block_ids, axis=1)]
    all_to_all x3 -> x0, waiting for transfers between devices: 20.2 us -> none  [the longest x1 16.7 us: body(): lax.all_to_all(outgoing, 'dict', split_axis=0, concat_axis=0, tiled=True)]
    all_to_all x3 -> x0, starting transfers between devices: 15.5 us -> none  [the longest x1 7.36 us: body(): lax.all_to_all(slot_flags, 'dict', split_axis=0, concat_axis=0, tiled=True)]
    dot_general x8 -> x0, matrix products: 12.5 us -> none  [the longest x1 2.53 us: body(): jnp.einsum('sbcl,sbcd->bld', latent, err_in, preferred_element_type=jnp.f...]
    unnamed x16 -> x6, local copies, waits for them, and re-layouts: 10.4 us -> 5.62 us
  transfers between devices with their start and end apart: 3 -> 0, of which waited for: 2 -> 0; matrix products, arithmetic and copies ran while one was open for 4% -> 0% of each run, Pallas kernels for 0% -> 0%
where the time goes in v1:
time: 90 us; the launch traced here: 89.5 us
  Pallas kernels  80.5 us (89%)
  local copies, waits for them, and re-layouts  8.28 us (9%)
    pallas_call x1, Pallas kernels, body(): pl.pallas_call(functools.partial(exchange_kernel, n, block_ids.shape[1]),...  74.3 us
    pallas_call x1, Pallas kernels, body(): pl.pallas_call(grad_kernel, grid=(2, tiles), out_shape=(jax.ShapeDtypeStr...  6.24 us
    unnamed x6, local copies, waits for them, and re-layouts  5.62 us

profile of v1, /device:TPU:0, one launch (start us, length us, event | category | flops | bytes accessed | tf_op | source)
XLA Modules:
  0.0 89.5 jit_solution(3452268904964655379)
XLA Ops:
  0.6 1.3 %reshape.22.dec_bias_ref = f32[1,3584]{1,0:T(1,128)} reshape(f32[3584]{0:T(1024)} %param.13) | data formatting | bytes 28672 | tf_op jit(solution)/shard_map/reshape | solution.py:326
  2.0 1.4 %copy.12.ids_ref = s32[128,32]{1,0:T(8,128)} copy(s32[128,32]{0,1:T(8,128)} %param.8) | data formatting | bytes 32768 | tf_op args[1]
  3.4 1.4 %copy.13.live_ref = s32[128,32]{1,0:T(8,128)} copy(s32[128,32]{0,1:T(8,128)} %param.9) | data formatting | bytes 32768 | tf_op args[2]
  4.9 74.3 %exchange.1 = (bf16[128,3584]{1,0:T(8,128)(2,1)}, bf16[256,1792]{1,0:T(8,128)(2,1)}, bf16[256,1792]{1,0:T(8,128)(2,1)}, bf16[256,256]{1,0:T(8,128)(2,1)}, bf16[2...) custom-call(s32[128,32]{1,0:T(8,128)} %copy.12.ids_ref, s32[128,32]{1,0:T(8,128)} %copy.13.live_ref, ...), custom_call_target="tpu_custom_call" | custom-call | tf_op jit(solution)/shard_map/exchange/pallas_call | solution.py:281
  79.1 0.0 copy-start
  79.2 0.7 slice.6
  79.9 0.6 slice.7
  80.5 6.2 %grads.1 = (f32[3584,256]{1,0:T(8,128)}, f32[256,3584]{1,0:T(8,128)}) custom-call(bf16[256,1792]{1,0:T(8,128)(2,1)} %get-tuple-element.15.rows_ref, bf16[256,1792]{1,0:T(8,128)(2,1)} %get-tuple-element.16.err_ref, bf16[256,256]{1,0:T(8,128)(2,1)} %get-tuple-element.17.lat_ref, bf16[256,256]{1,0:T(8,128)(2,1)} %get-tuple-element.18.dlat_ref), custom_call_target="tpu_custom_call" | custom-call | tf_op jit(solution)/shard_map/grads/pallas_call | solution.py:332
  86.7 2.2 %copy.18 = bf16[128,3584]{1,0:T(8,128)(2,1)} copy(bf16[128,3584]{1,0:T(8,128)(2,1)} %get-tuple-element.28) | data formatting | bytes 1835008
  88.9 0.0 copy-done
  88.9 0.6 copy.19
Async XLA Ops:
  79.1 9.8 %copy-start = (f32[1,256]{1,0:T(1,128)S(1)}, f32[1,256]{1,0:T(1,128)}, u32[]{:S(2)}) copy-start(f32[1,256]{1,0:T(1,128)} %get-tuple-element.20) | copy-start | bytes 3076

commit v2 on v1

v2 whole, which is shorter than its diff:
```python
import functools

import jax
import jax.numpy as jnp
from jax import lax
from jax.experimental import pallas as pl
from jax.experimental.pallas import tpu as pltpu
from jax.sharding import PartitionSpec as P

BLOCK = 64
CAP = 2
ROW_DEV = 128
SCALE = 1.0 / ROW_DEV
LANES = 128
TILES = 2
VMEM_LIMIT = 58 * 1024 * 1024
F32 = jnp.float32
BF16 = jnp.bfloat16


def chunk_list(half):
    units = half // LANES
    parts = [4, 4, 4] if units > 12 else []
    rest = units - sum(parts)
    parts = ([rest] if rest else []) + parts
    out, start = [], 0
    for part in parts:
        out.append((start * LANES, part * LANES))
        start += part
    return out


def dot(a, b):
    return jnp.dot(a, b, preferred_element_type=F32)


def dot_nt(a, b):
    return lax.dot_general(a, b, (((1,), (1,)), ((), ())), preferred_element_type=F32)


def dot_tn(a, b):
    return lax.dot_general(a, b, (((0,), (0,)), ((), ())), preferred_element_type=F32)


def exchange_kernel(
    n, ids_ref, live_ref, enc_bias_ref, dec_bias_ref, act_hbm, enc_hbm, dec_hbm,
    recon_hbm, rows_hbm, err_hbm, lat_ref, dlat_ref, enc_grad_ref, sum_ref,
    act, recon, enc, dec, out_buf, rows_in, term_out, term_in, err_in, pick, pick_t, part, part_in,
    load_sem, store_sem, send1, recv1, send2, recv2, send3, recv3, send4, recv4,
):
    me = lax.axis_index("dict")
    rows_total = 16 * n
    slots = ids_ref.shape[0]
    rows = ids_ref.shape[1]
    half = act.shape[1]
    width = BLOCK * 4
    chunks = chunk_list(half)
    bits = [1 << k for k in range(n.bit_length() - 1)]

    def peer_of(step):
        index = n - step
        return sum(((me // bit + index // bit) % 2) * bit for bit in bits)

    def for_peers(fn, low=1, high=n):
        def step_fn(step, carry):
            fn(peer_of(step))
            return carry

        lax.fori_loop(low, high, step_fn, 0)

    quarter = n // 4
    mine_quarter = me // quarter
    groups = [
        ((3 - mine_quarter) * quarter, quarter, 1, quarter + 1),
        (((mine_quarter + 2) % 4) * quarter, quarter, quarter + 1, 2 * quarter + 1),
        ((me // (2 * quarter)) * 2 * quarter, 2 * quarter, 2 * quarter + 1, n),
    ]

    act_low = pltpu.make_async_copy(
        act_hbm.at[:, pl.ds(0, half)], act.at[pl.ds(0, rows)], load_sem.at[2]
    )
    act_high = pltpu.make_async_copy(
        act_hbm.at[:, pl.ds(half, half)], act.at[pl.ds(rows, rows)], load_sem.at[3]
    )
    enc_load = pltpu.make_async_copy(enc_hbm, enc, load_sem.at[0])
    dec_load = pltpu.make_async_copy(dec_hbm, dec, load_sem.at[1])
    act_low.start()
    act_high.start()
    enc_load.start()
    dec_load.start()
    barrier = pltpu.get_barrier_semaphore()
    for_peers(
        lambda peer: pl.semaphore_signal(
            barrier, inc=1, device_id={"dict": peer}, device_id_type=pl.DeviceIdType.MESH
        )
    )

    def block_rows(device, count=1):
        return pl.ds(pl.multiple_of(device * 16, 16), count * 16)

    def send(src, dst, start, size, send_sem, recv_sem, low=1, high=n):
        mine = block_rows(me)
        columns = pl.ds(start, size)

        def one(peer):
            pltpu.make_async_remote_copy(
                src_ref=src.at[block_rows(peer), columns],
                dst_ref=dst.at[mine, columns],
                send_sem=send_sem,
                recv_sem=recv_sem,
                device_id={"dict": peer},
                device_id_type=pl.DeviceIdType.MESH,
            ).start()

        for_peers(one, low, high)
        if high == n:
            dst[mine, columns] = src[mine, columns]

    def wait_all(buf, start, size, sem, count=n - 1):
        view = buf.at[pl.ds(0, count * 16), pl.ds(start, size)]
        pltpu.make_async_copy(view, view, sem).wait()

    column = lax.broadcasted_iota(jnp.int32, (slots, rows_total), 1)
    block = (column // 16) * 4 + (column % 8) // CAP
    per_slot = 4 * n // slots
    spread = (
        lax.broadcasted_iota(jnp.int32, (slots, rows_total), 0) == block // per_slot
    ).astype(F32).astype(BF16)
    slot_base = lax.broadcasted_iota(jnp.int32, (slots, rows), 0) * per_slot
    code = jnp.where(live_ref[...] == 1, ids_ref[...] - slot_base + 1, 0).astype(F32)
    code = dot_tn(code.astype(BF16), spread)
    column = lax.broadcasted_iota(jnp.int32, (rows, rows_total), 1)
    block = (column // 16) * 4 + (column % 8) // CAP
    hit = code == (block % per_slot + 1).astype(F32)
    lower = (
        lax.broadcasted_iota(jnp.int32, (rows, rows), 1)
        < lax.broadcasted_iota(jnp.int32, (rows, rows), 0)
    ).astype(F32).astype(BF16)
    earlier = dot(lower, hit.astype(F32).astype(BF16))
    chosen = hit & (earlier == (column % CAP).astype(F32))
    top = (column // 8) % 2
    pick_low = jnp.where(chosen & (top == 0), 1.0, 0.0)
    pick_high = jnp.where(chosen & (top == 1), 1.0, 0.0)
    both = jnp.concatenate([pick_low, pick_high], axis=0)
    pick[...] = both.astype(BF16)
    pick_t[...] = both.T.astype(BF16)
    part[...] = jnp.zeros_like(part)

    act_low.wait()
    act_high.wait()
    for g, (first, count, low, high) in enumerate(groups):
        group_rows = block_rows(first, count)
        for start, size in chunks:
            columns = pl.ds(start, size)
            out_buf[group_rows, columns] = dot(pick_t[group_rows, :], act[:, columns]).astype(BF16)
        if g == 0:
            pl.semaphore_wait(barrier, n - 1)
        send(out_buf, rows_in, 0, half, send1, recv1.at[g], low, high)
    enc_load.wait()
    dec_load.wait()

    def stack(value):
        count = value.shape[0]
        value = jnp.broadcast_to(value[:, None], (count, 2, 8, width))
        return value.reshape(16 * count, width)

    for g, (first, count, low, high) in enumerate(groups):
        group_rows = block_rows(first, count)
        wait_all(rows_in, 0, half, recv1.at[g], count - (1 if high == n else 0))
        value = rows_in[group_rows, :]
        first_half = dot(value, enc[:half, :]).reshape(count, 2, 8, width)
        last_half = dot(value, enc[half:, :]).reshape(count, 2, 8, width)
        preact = first_half[:, 0] + last_half[:, 1] + enc_bias_ref[...].reshape(1, 1, width)
        own_block = (
            lax.broadcasted_iota(jnp.int32, (count, 8, width), 1) // CAP
            == lax.broadcasted_iota(jnp.int32, (count, 8, width), 2) // BLOCK
        )
        latent = stack(jnp.where(own_block, jnp.maximum(preact, 0.0), 0.0))
        lat_ref[group_rows, :] = latent.astype(BF16)
        top = (lax.broadcasted_iota(jnp.int32, latent.shape, 0) // 8) % 2
        latent_low = jnp.where(top == 0, latent, 0.0).astype(BF16)
        latent_high = jnp.where(top == 1, latent, 0.0).astype(BF16)
        for c, (start, size) in enumerate(chunks):
            value = dot(latent_low, dec[:, start : start + size])
            value = value + dot(latent_high, dec[:, half + start : half + start + size])
            term_out[group_rows, start : start + size] = value.astype(BF16)
            send(term_out, term_in, start, size, send2.at[c], recv2.at[c], low, high)

    rows_store = pltpu.make_async_copy(rows_in, rows_hbm, store_sem.at[0])
    rows_store.start()
    wait_all(out_buf, 0, half, send1)

    units_per = part.shape[1]
    for c, (start, size) in enumerate(chunks):
        columns = pl.ds(start, size)
        wait_all(term_in, start, size, recv2.at[c])
        combined = dot(pick[...], term_in[:, columns])
        errors = []
        for h in range(2):
            unit = (h * half + start) // LANES
            bias = jnp.concatenate(
                [dec_bias_ref[unit + u : unit + u + 1, :] for u in range(size // LANES)], axis=1
            )
            residual = combined[h * rows : (h + 1) * rows] + bias
            residual = residual - act[h * rows : (h + 1) * rows, columns].astype(F32)
            errors.append(residual.astype(BF16))
            total = SCALE * jnp.sum(residual, axis=0, keepdims=True)
            for u in range(size // LANES):
                part[(unit + u) // units_per, (unit + u) % units_per, :] = total[
                    0, u * LANES : (u + 1) * LANES
                ]
        error = jnp.concatenate(errors, axis=0)
        recon[:, columns] = error
        out_buf[:, columns] = dot(pick_t[...], error).astype(BF16)
        send(out_buf, err_in, start, size, send3.at[c], recv3.at[c])
    recon_store = pltpu.make_async_copy(recon, recon_hbm, store_sem.at[1])
    recon_store.start()

    def send_part(peer):
        pltpu.make_async_remote_copy(
            src_ref=part.at[peer],
            dst_ref=part_in.at[me],
            send_sem=send4.at[0],
            recv_sem=recv4.at[0],
            device_id={"dict": peer},
            device_id_type=pl.DeviceIdType.MESH,
        ).start()

    for_peers(send_part)
    part_in[me] = part[me]

    def wait_parts(buf, sem):
        view = buf.at[pl.ds(0, n - 1)]
        pltpu.make_async_copy(view, view, sem).wait()

    def send_total(peer):
        pltpu.make_async_remote_copy(
            src_ref=sum_ref.at[me],
            dst_ref=sum_ref.at[me],
            send_sem=send4.at[1],
            recv_sem=recv4.at[1],
            device_id={"dict": peer},
            device_id_type=pl.DeviceIdType.MESH,
        ).start()

    first_half = jnp.zeros((rows_total, width), F32)
    last_half = jnp.zeros((rows_total, width), F32)
    stores = []
    for c, (start, size) in enumerate(chunks):
        if c == len(chunks) - 1:
            wait_parts(part_in, recv4.at[0])
            wait_parts(part, send4.at[0])
            sum_ref[me] = jnp.sum(part_in[...], axis=0)
            for_peers(send_total)
        wait_all(err_in, start, size, recv3.at[c])
        columns = pl.ds(start, size)
        store = pltpu.make_async_copy(
            err_in.at[:, columns], err_hbm.at[:, columns], store_sem.at[2 + c]
        )
        store.start()
        stores.append(store)
        value = err_in[:, columns]
        first_half = first_half + dot_nt(value, dec[:, start : start + size])
        last_half = last_half + dot_nt(value, dec[:, half + start : half + start + size])
    first_half = first_half.reshape(n, 2, 8, width)
    last_half = last_half.reshape(n, 2, 8, width)
    latent = lat_ref[...].astype(F32).reshape(n, 2, 8, width)[:, 0]
    dlatent = jnp.where(latent > 0, SCALE * (first_half[:, 0] + last_half[:, 1]), 0.0)
    enc_grad_ref[...] = jnp.sum(dlatent.reshape(n * 8, width), axis=0, keepdims=True)
    dlat_ref[...] = stack(dlatent).astype(BF16)

    for c, (start, size) in enumerate(chunks):
        wait_all(term_out, start, size, send2.at[c])
        wait_all(out_buf, start, size, send3.at[c])
        stores[c].wait()
    rows_store.wait()
    recon_store.wait()
    wait_parts(sum_ref, recv4.at[1])
    wait_parts(sum_ref, send4.at[1])


def grad_kernel(
    rows_ref, err_ref, lat_ref, dlat_ref, recon_ref, bias_ref, sum_ref,
    enc_out, dec_out, recon_out, bias_out, sum_out,
):
    h = pl.program_id(1)

    @pl.when((pl.program_id(0) == 0) & (h == 0))
    def _():
        bias_out[...] = bias_ref[...]
        per = sum_ref.shape[1]
        for unit in range(sum_out.shape[0]):
            sum_out[unit, :] = sum_ref[unit // per, unit % per, :]

    top = (lax.broadcasted_iota(jnp.int32, lat_ref.shape, 0) // 8) % 2
    keep = top == h
    latent = jnp.where(keep, lat_ref[...].astype(F32), 0.0).astype(BF16)
    dlatent = jnp.where(keep, dlat_ref[...].astype(F32), 0.0).astype(BF16)
    enc_out[...] = dot_tn(rows_ref[...], dlatent)
    dec_out[...] = SCALE * dot_tn(latent, err_ref[...])
    recon_out[...] = recon_ref[...]


def body(activations, block_ids, slot_mask, enc_weight, enc_bias, dec_weight, dec_bias):
    n = lax.axis_size("dict")
    rows, model_width = activations.shape
    half = model_width // 2
    width = enc_bias.shape[0]
    rows_total = 16 * n
    units = model_width // LANES
    units_per = -(-units // n)
    chunks = len(chunk_list(half))
    vmem = pl.BlockSpec(memory_space=pltpu.VMEM)
    hbm = pl.BlockSpec(memory_space=pl.ANY)
    slot_buf = pltpu.VMEM((rows_total, half), BF16)
    recon_error, rows_in, err_in, latent, dlatent, enc_bias_grad, sums = pl.pallas_call(
        functools.partial(exchange_kernel, n),
        out_shape=(
            jax.ShapeDtypeStruct((2 * rows, half), BF16),
            jax.ShapeDtypeStruct((rows_total, half), BF16),
            jax.ShapeDtypeStruct((rows_total, half), BF16),
            jax.ShapeDtypeStruct((rows_total, width), BF16),
            jax.ShapeDtypeStruct((rows_total, width), BF16),
            jax.ShapeDtypeStruct((1, width), F32),
            jax.ShapeDtypeStruct((n, units_per, LANES), F32),
        ),
        in_specs=[vmem] * 4 + [hbm] * 3,
        out_specs=(hbm, hbm, hbm, vmem, vmem, vmem, vmem),
        scratch_shapes=[
            pltpu.VMEM((2 * rows, half), BF16),
            pltpu.VMEM((2 * rows, half), BF16),
            pltpu.VMEM((model_width, width), BF16),
            pltpu.VMEM((width, model_width), BF16),
            slot_buf,
            slot_buf,
            slot_buf,
            slot_buf,
            slot_buf,
            pltpu.VMEM((2 * rows, rows_total), BF16),
            pltpu.VMEM((rows_total, 2 * rows), BF16),
            pltpu.VMEM((n, units_per, LANES), F32),
            pltpu.VMEM((n, units_per, LANES), F32),
            pltpu.SemaphoreType.DMA((4,)),
            pltpu.SemaphoreType.DMA((2 + chunks,)),
            pltpu.SemaphoreType.DMA,
            pltpu.SemaphoreType.DMA((3,)),
            pltpu.SemaphoreType.DMA((chunks,)),
            pltpu.SemaphoreType.DMA((chunks,)),
            pltpu.SemaphoreType.DMA((chunks,)),
            pltpu.SemaphoreType.DMA((chunks,)),
            pltpu.SemaphoreType.DMA((2,)),
            pltpu.SemaphoreType.DMA((2,)),
        ],
        compiler_params=pltpu.CompilerParams(
            collective_id=0, has_side_effects=True, vmem_limit_bytes=VMEM_LIMIT
        ),
        name="exchange",
    )(
        block_ids.T,
        slot_mask.T,
        enc_bias.reshape(1, width),
        dec_bias.reshape(units, LANES),
        activations,
        enc_weight,
        dec_weight,
    )
    tiles = TILES
    tile = half // tiles
    grad_enc, grad_dec, recon_error, enc_bias_grad, sums = pl.pallas_call(
        grad_kernel,
        grid=(tiles, 2),
        out_shape=(
            jax.ShapeDtypeStruct((model_width, width), F32),
            jax.ShapeDtypeStruct((width, model_width), F32),
            jax.ShapeDtypeStruct((rows, model_width), BF16),
            jax.ShapeDtypeStruct((1, width), F32),
            jax.ShapeDtypeStruct((units, LANES), F32),
        ),
        in_specs=[
            pl.BlockSpec((rows_total, tile), lambda j, h: (0, j)),
            pl.BlockSpec((rows_total, tile), lambda j, h: (0, j)),
            pl.BlockSpec((rows_total, width), lambda j, h: (0, 0)),
            pl.BlockSpec((rows_total, width), lambda j, h: (0, 0)),
            pl.BlockSpec((rows, tile), lambda j, h: (h, j)),
            pl.BlockSpec((1, width), lambda j, h: (0, 0)),
            pl.BlockSpec((n, units_per, LANES), lambda j, h: (0, 0, 0)),
        ],
        out_specs=(
            pl.BlockSpec((tile, width), lambda j, h: (h * tiles + j, 0)),
            pl.BlockSpec((width, tile), lambda j, h: (0, h * tiles + j)),
            pl.BlockSpec((rows, tile), lambda j, h: (0, h * tiles + j)),
            pl.BlockSpec((1, width), lambda j, h: (0, 0)),
            pl.BlockSpec((units, LANES), lambda j, h: (0, 0)),
        ),
        compiler_params=pltpu.CompilerParams(vmem_limit_bytes=VMEM_LIMIT),
        name="grads",
    )(rows_in, err_in, latent, dlatent, recon_error, enc_bias_grad, sums)
    return (
        recon_error,
        grad_enc,
        enc_bias_grad.reshape(width),
        grad_dec,
        sums.reshape(model_width),
    )


def solution(mesh):
    return jax.shard_map(
        body,
        mesh=mesh,
        in_specs=(
            P(("groups", "dict"), None),
            P(("groups", "dict"), None),
            P(("groups", "dict"), None),
            P(None, "dict"),
            P("dict"),
            P("dict", None),
            P(),
        ),
        out_specs=(
            P(("groups", "dict"), None),
            P("groups", "dict"),
            P(("groups", "dict")),
            P(("groups", "dict"), None),
            P("groups"),
        ),
        check_vma=False,
    )
```

time: 90 us -> 81 us (0.900)
  local copies, waits for them, and re-layouts: 8.28 us -> 0 us
    unnamed x6 -> x0, local copies, waits for them, and re-layouts: 5.62 us -> none
    slice x2 -> x0, local copies, waits for them, and re-layouts: 1.34 us -> none  [body(): sums.reshape(n * units_per * LANES)[:model_width]]
    reshape x1 -> x0, local copies, waits for them, and re-layouts: 1.33 us -> none  [body(): dec_bias.reshape(1, model_width)]
where the time goes in v2:
time: 81 us; the launch traced here: 80.7 us
  Pallas kernels  80 us (99%)
    pallas_call x1, Pallas kernels, body(): pl.pallas_call(functools.partial(exchange_kernel, n), out_shape=(jax.Shap...  73.6 us
    pallas_call x1, Pallas kernels, body(): pl.pallas_call(grad_kernel, grid=(tiles, 2), out_shape=(jax.ShapeDtypeStr...  6.42 us

profile of v2, /device:TPU:0, one launch (start us, length us, event | category | flops | bytes accessed | tf_op | source)
XLA Modules:
  0.0 80.7 jit_solution(15969239289156300210)
XLA Ops:
  0.6 73.6 %exchange.1 = (bf16[256,1792]{1,0:T(8,128)(2,1)}, bf16[256,1792]{1,0:T(8,128)(2,1)}, bf16[256,1792]{1,0:T(8,128)(2,1)}, bf16[256,256]{1,0:T(8,128)(2,1)}, bf16[2...) custom-call(s32[32,128]{1,0:T(8,128)} %bitcast.6, s32[32,128]{1,0:T(8,128)} %bitcast.7, ...), custom_call_target="tpu_custom_call" | custom-call | tf_op jit(solution)/shard_map/exchange/pallas_call | solution.py:316
  74.2 6.4 %grads.1 = (f32[3584,256]{1,0:T(8,128)}, f32[256,3584]{1,0:T(8,128)}, bf16[128,3584]{1,0:T(8,128)(2,1)}, f32[1,256]{1,0:T(1,128)}, f32[28,128]{1,0:T(8,128)}) custom-call(bf16[256,1792]{1,0:T(8,128)(2,1)} %get-tuple-element.17.rows_ref, bf16[256,1792]{1,0:T(8,128)(2,1)} %get-tuple-element.18.err_ref, bf16[256,256]{1,0:T(8,128)(2,1)} %get-tuple-element.19.lat_ref, ...), custom_call_target="tpu_custom_call" | custom-call | tf_op jit(solution)/shard_map/grads/pallas_call | solution.py:369

commit v3 on v2

--- a/solution.py
+++ b/solution.py
@@ -86,8 +86,6 @@
     dec_load = pltpu.make_async_copy(dec_hbm, dec, load_sem.at[1])
     act_low.start()
     act_high.start()
-    enc_load.start()
-    dec_load.start()
     barrier = pltpu.get_barrier_semaphore()
     for_peers(
         lambda peer: pl.semaphore_signal(
@@ -148,6 +146,8 @@
 
     act_low.wait()
     act_high.wait()
+    enc_load.start()
+    dec_load.start()
     for g, (first, count, low, high) in enumerate(groups):
         group_rows = block_rows(first, count)
         for start, size in chunks:
@@ -190,6 +190,16 @@
     rows_store.start()
     wait_all(out_buf, 0, half, send1)
 
+    def send_part(peer):
+        pltpu.make_async_remote_copy(
+            src_ref=part.at[peer],
+            dst_ref=part_in.at[me],
+            send_sem=send4.at[0],
+            recv_sem=recv4.at[0],
+            device_id={"dict": peer},
+            device_id_type=pl.DeviceIdType.MESH,
+        ).start()
+
     units_per = part.shape[1]
     for c, (start, size) in enumerate(chunks):
         columns = pl.ds(start, size)
@@ -209,25 +219,15 @@
                 part[(unit + u) // units_per, (unit + u) % units_per, :] = total[
                     0, u * LANES : (u + 1) * LANES
                 ]
+        if c == len(chunks) - 1:
+            for_peers(send_part)
+            part_in[me] = part[me]
         error = jnp.concatenate(errors, axis=0)
         recon[:, columns] = error
         out_buf[:, columns] = dot(pick_t[...], error).astype(BF16)
         send(out_buf, err_in, start, size, send3.at[c], recv3.at[c])
     recon_store = pltpu.make_async_copy(recon, recon_hbm, store_sem.at[1])
     recon_store.start()
-
-    def send_part(peer):
-        pltpu.make_async_remote_copy(
-            src_ref=part.at[peer],
-            dst_ref=part_in.at[me],
-            send_sem=send4.at[0],
-            recv_sem=recv4.at[0],
-            device_id={"dict": peer},
-            device_id_type=pl.DeviceIdType.MESH,
-        ).start()
-
-    for_peers(send_part)
-    part_in[me] = part[me]
 
     def wait_parts(buf, sem):
         view = buf.at[pl.ds(0, n - 1)]

time: 81 us -> 78.7 us (0.972)
  Pallas kernels: 80 us -> 77.7 us
    pallas_call x1, Pallas kernels: 73.6 us -> 71.3 us  [body(): pl.pallas_call(functools.partial(exchange_kernel, n), out_shape=(jax.Shap...]
where the time goes in v3:
time: 78.7 us; the launch traced here: 78.4 us
  Pallas kernels  77.7 us (99%)
    pallas_call x1, Pallas kernels, body(): pl.pallas_call(functools.partial(exchange_kernel, n), out_shape=(jax.Shap...  71.3 us
    pallas_call x1, Pallas kernels, body(): pl.pallas_call(grad_kernel, grid=(tiles, 2), out_shape=(jax.ShapeDtypeStr...  6.42 us

profile of v3, /device:TPU:0, one launch (start us, length us, event | category | flops | bytes accessed | tf_op | source)
XLA Modules:
  0.0 78.4 jit_solution(2522001915637864815)
XLA Ops:
  0.6 71.3 %exchange.1 = (bf16[256,1792]{1,0:T(8,128)(2,1)}, bf16[256,1792]{1,0:T(8,128)(2,1)}, bf16[256,1792]{1,0:T(8,128)(2,1)}, bf16[256,256]{1,0:T(8,128)(2,1)}, bf16[2...) custom-call(s32[32,128]{1,0:T(8,128)} %bitcast.6, s32[32,128]{1,0:T(8,128)} %bitcast.7, ...), custom_call_target="tpu_custom_call" | custom-call | tf_op jit(solution)/shard_map/exchange/pallas_call | solution.py:316
  72.0 6.4 %grads.1 = (f32[3584,256]{1,0:T(8,128)}, f32[256,3584]{1,0:T(8,128)}, bf16[128,3584]{1,0:T(8,128)(2,1)}, f32[1,256]{1,0:T(1,128)}, f32[28,128]{1,0:T(8,128)}) custom-call(bf16[256,1792]{1,0:T(8,128)(2,1)} %get-tuple-element.17.rows_ref, bf16[256,1792]{1,0:T(8,128)(2,1)} %get-tuple-element.18.err_ref, bf16[256,256]{1,0:T(8,128)(2,1)} %get-tuple-element.19.lat_ref, ...), custom_call_target="tpu_custom_call" | custom-call | tf_op jit(solution)/shard_map/grads/pallas_call | solution.py:369

commit v4 on v3

--- a/solution.py
+++ b/solution.py
@@ -12,7 +12,7 @@
 ROW_DEV = 128
 SCALE = 1.0 / ROW_DEV
 LANES = 128
-TILES = 2
+TILES = 1
 VMEM_LIMIT = 58 * 1024 * 1024
 F32 = jnp.float32
 BF16 = jnp.bfloat16
@@ -20,7 +20,7 @@
 
 def chunk_list(half):
     units = half // LANES
-    parts = [4, 4, 4] if units > 12 else []
+    parts = [5, 5] if units > 12 else []
     rest = units - sum(parts)
     parts = ([rest] if rest else []) + parts
     out, start = [], 0

time: 78.7 us -> 77.3 us (0.982)
  Pallas kernels: 77.7 us -> 76.3 us
where the time goes in v4:
time: 77.3 us; the launch traced here: 76.9 us
  Pallas kernels  76.3 us (99%)
    pallas_call x1, Pallas kernels, body(): pl.pallas_call(functools.partial(exchange_kernel, n), out_shape=(jax.Shap...  70.6 us
    pallas_call x1, Pallas kernels, body(): pl.pallas_call(grad_kernel, grid=(tiles, 2), out_shape=(jax.ShapeDtypeStr...  5.72 us

profile of v4, /device:TPU:0, one launch (start us, length us, event | category | flops | bytes accessed | tf_op | source)
XLA Modules:
  0.0 76.9 jit_solution(10460652056732712859)
XLA Ops:
  0.6 70.6 %exchange.1 = (bf16[256,1792]{1,0:T(8,128)(2,1)}, bf16[256,1792]{1,0:T(8,128)(2,1)}, bf16[256,1792]{1,0:T(8,128)(2,1)}, bf16[256,256]{1,0:T(8,128)(2,1)}, bf16[2...) custom-call(s32[32,128]{1,0:T(8,128)} %bitcast.6, s32[32,128]{1,0:T(8,128)} %bitcast.7, ...), custom_call_target="tpu_custom_call" | custom-call | tf_op jit(solution)/shard_map/exchange/pallas_call | solution.py:316
  71.2 5.7 %grads.1 = (f32[3584,256]{1,0:T(8,128)}, f32[256,3584]{1,0:T(8,128)}, bf16[128,3584]{1,0:T(8,128)(2,1)}, f32[1,256]{1,0:T(1,128)}, f32[28,128]{1,0:T(8,128)}) custom-call(bf16[256,1792]{1,0:T(8,128)(2,1)} %get-tuple-element.17.rows_ref, bf16[256,1792]{1,0:T(8,128)(2,1)} %get-tuple-element.18.err_ref, bf16[256,256]{1,0:T(8,128)(2,1)} %get-tuple-element.19.lat_ref, ...), custom_call_target="tpu_custom_call" | custom-call | tf_op jit(solution)/shard_map/grads/pallas_call | solution.py:369
